TPU v7x, 32 devices: a whole 2x2x4 slice. The times are simulated.
32 devices in a mesh: fsdp: 8 (over y, x, core), tensor: 4 (over z).
Axes of the slice: x: 2, y: 2, z: 4, core: 2. Of those that a mesh axis runs over, the one named last changes fastest.
Arguments:
- tokens: bfloat16 [1024, 16384], P('fsdp', 'tensor'), may hold values from -6 to 6
- seg_ids: int32 [8, 128], P('fsdp'), may hold values from 0 to 7, never falling along the last dimension, each value on 1 to 64 neighbouring positions
- key_weight: bfloat16 [512, 16384], P('fsdp', 'tensor'), may hold values from -0.046875 to 0.046875
- key_grad: bfloat16 [1024, 512], P('fsdp'), may hold values from -6 to 6
Outputs:
- keys: bfloat16 [1024, 512], P('fsdp')
- grad_tokens: bfloat16 [1024, 16384], P('fsdp', 'tensor')
- grad_key_weight: float32 [512, 16384], P('fsdp', 'tensor')
Inputs may be any that keep to these rules, and one draw needn't show every extreme that they name: `seg_ids`: within each window the ids never fall; each document spans 1 to 64 tokens, one exactly 64.
All inputs are finite; a program needn't handle non-finite values.
Results may differ from a plain program's by a relative error of at most 0.0041.
Values may be sent and summed in bfloat16 or wider, within the bound.
A program may use at most 64 MiB of HBM per device.

v0:
```python
import jax
import jax.numpy as jnp
from jax import lax
from jax.sharding import PartitionSpec as P

HEAD = 128


def doc_positions(segments):
    width = segments.shape[0]
    index = jnp.arange(width, dtype=jnp.int32)
    change = jnp.concatenate([jnp.ones((1,), bool), segments[1:] != segments[:-1]])
    first = lax.cummax(jnp.where(change, index, 0))
    return index - first


def angles(positions, half):
    freq = 500000.0 ** (-2.0 * jnp.arange(half, dtype=jnp.float32) / (2 * half))
    turn = positions.astype(jnp.float32)[:, None] * freq[None, :]
    return (jnp.cos(turn)[:, None, :], jnp.sin(turn)[:, None, :])


def rotate(field, cosine, sine, sign):
    rows = field.shape[0]
    shaped = field.reshape(rows, -1, HEAD)
    first, second = (shaped[..., : HEAD // 2], shaped[..., HEAD // 2 :])
    out = jnp.concatenate(
        [first * cosine - sign * second * sine, second * cosine + sign * first * sine], axis=-1
    )
    return out.reshape(rows, -1)


def body(tokens, seg_ids, key_weight, key_grad):
    cosine, sine = angles(doc_positions(seg_ids[0]), HEAD // 2)
    weights = lax.all_gather(key_weight, "fsdp", axis=0, tiled=True)
    partial_value = lax.dot_general(
        tokens, weights, (((1,), (1,)), ((), ())), preferred_element_type=jnp.float32
    )
    kraw = lax.psum(partial_value, "tensor")
    keys = rotate(kraw, cosine, sine, 1.0).astype(jnp.bfloat16)
    kback = rotate(key_grad.astype(jnp.float32), cosine, sine, -1.0).astype(jnp.bfloat16)
    grad_tokens = jnp.dot(kback, weights, preferred_element_type=jnp.float32)
    grad_key_weight = lax.psum_scatter(
        lax.dot_general(
            kback, tokens, (((0,), (0,)), ((), ())), preferred_element_type=jnp.float32
        ),
        "fsdp",
        scatter_dimension=0,
        tiled=True,
    )
    return (keys, grad_tokens.astype(jnp.bfloat16), grad_key_weight)


def solution(mesh):
    placed = (P("fsdp", "tensor"), P("fsdp", None), P("fsdp", "tensor"), P("fsdp", None))
    return jax.shard_map(
        body,
        mesh=mesh,
        in_specs=placed,
        out_specs=(P("fsdp", None), P("fsdp", "tensor"), P("fsdp", "tensor")),
        check_vma=False,
    )
```

profile of v0, /device:TPU:0, one launch (start us, length us, event | category | flops | bytes accessed | tf_op | source)
XLA Modules:
  0.0 173.5 jit_solution(18427366690524540398)
XLA Ops:
  7.2 0.0 copy-start
  7.2 0.0 copy-start.1
  7.2 0.0 all-gather.2.cloned.1.call-start
  7.2 0.7 all-gather.2.cloned.1.call-update
  7.9 0.0 all-reduce.2.cloned.1.call-start
  8.0 0.8 compare_bitcast_fusion
  8.8 0.1 add_select_fusion
  8.9 0.1 copy.8
  9.0 0.2 reduce-window.8
  9.1 0.1 reduce
  9.3 40.1 %all-gather.2.cloned.1.call-done = bf16[512,4096]{1,0:T(8,128)(2,1)} async-done(((bf16[64,4096]{1,0:T(8,128)(2,1)}), bf16[512,4096]{1,0:T(8,128)(2,1)}) %all-gather.2.cloned.1.call-update) | async-done | bytes 4194320 | tf_op jit(solution)/shard_map/all_gather | solution.py:35
  49.4 0.0 copy-done
  49.4 3.7 %fusion.5 = f32[128,512]{1,0:T(8,128)S(1)} fusion(bf16[128,4096]{1,0:T(8,128)(2,1)S(1)} %copy-done, bf16[512,4096]{1,0:T(8,128)(2,1)} %all-gather.2.cloned.1.call-done), kind=kOutput, calls=%fused_computation.20 | convolution fusion | flops 536870912 | bytes 5505024 | tf_op jit(solution)/shard_map/dot_general | solution.py:36
  53.1 0.8 reshape.134
  53.9 0.0 all-reduce.2.cloned.1.call-update
  53.9 0.0 reduce-scatter.2.cloned.1.call-start
  54.0 0.0 copy-done.1
  54.0 0.1 reshape.139
  54.1 0.3 broadcast_multiply_fusion
  54.4 35.0 %all-reduce.2.cloned.1.call-done = f32[128,4,128]{2,1,0:T(4,128)} async-done(((f32[128,4,128]{2,1,0:T(4,128)}), f32[128,4,128]{2,1,0:T(4,128)}) %all-reduce.2.cloned.1.call-update) | async-done | bytes 262160 | tf_op jit(solution)/shard_map/psum | solution.py:39
  89.4 1.5 subtract_convert_fusion
  90.9 0.4 pad_maximum_fusion
  91.2 4.5 %fusion = f32[512,4096]{1,0:T(8,128)} fusion(bf16[128,4096]{1,0:T(8,128)(2,1)S(1)} %copy-done, bf16[16,8,4,128]{3,2,1,0:T(4,128)(2,1)S(1)} %bitcast.16), kind=kOutput, calls=%fused_computation.5 | convolution fusion | flops 536870912 | bytes 9568256 | tf_op jit(solution)/shard_map/dot_general | solution.py:44
  95.7 0.0 reduce-scatter.2.cloned.1.call-update
  95.8 0.7 copy.20
  96.4 3.9 %convolution_convert_fusion = bf16[128,4096]{1,0:T(8,128)(2,1)} fusion(bf16[512,4096]{1,0:T(8,128)(2,1)} %all-gather.2.cloned.1.call-done, bf16[16,8,4,128]{3,2,1,0:T(4,128)(2,1)S(1)} %bitcast.17), kind=kOutput, calls=%fused_computation | convolution fusion | flops 537395200 | bytes 5373952 | tf_op jit(solution)/shard_map/dot_general | solution.py:42
  100.3 66.6 %reduce-scatter.2.cloned.1.call-done = f32[64,4096]{1,0:T(8,128)} async-done(((f32[512,4096]{1,0:T(8,128)}), f32[64,4096]{1,0:T(8,128)}) %reduce-scatter.2.cloned.1.call-update) | async-done | bytes 1048592 | tf_op jit(solution)/shard_map/reduce_scatter | solution.py:43
  (2 shorter events, 0.0 us)
Async XLA Ops:
  7.2 42.2 %copy-start = (bf16[128,4096]{1,0:T(8,128)(2,1)S(1)}, bf16[128,4096]{1,0:T(8,128)(2,1)}, u32[]{:S(2)}) copy-start(bf16[128,4096]{1,0:T(8,128)(2,1)} %param.4) | copy-start | bytes 3145732
  7.2 46.8 %copy-start.1 = (bf16[128,512]{1,0:T(8,128)(2,1)S(1)}, bf16[128,512]{1,0:T(8,128)(2,1)}, u32[]{:S(2)}) copy-start(bf16[128,512]{1,0:T(8,128)(2,1)} %param.7) | copy-start | bytes 393220
  7.2 42.2 %all-gather.2.cloned.1.call-start = ((), (), s32[]{:S(2)}) async-start(), calls=%async_computation.1 | async-start | bytes 4718592 | tf_op jit(solution)/shard_map/all_gather | solution.py:35
  7.9 81.4 %all-reduce.2.cloned.1.call-start = ((), (), s32[]{:S(2)}) async-start(), calls=%async_computation.2 | async-start | bytes 524288 | tf_op jit(solution)/shard_map/psum | solution.py:39
  53.9 113.0 %reduce-scatter.2.cloned.1.call-start = ((), (), s32[]{:S(2)}) async-start(), calls=%async_computation.3 | async-start | bytes 9437184 | tf_op jit(solution)/shard_map/reduce_scatter | solution.py:43
Sparse Core Ops, SparseCore 0:
  9.9 39.4 all-gather.1
  54.0 35.2 all-reduce.1
  95.9 71.0 reduce-scatter.1
where the time goes:
time: 174 us; the launch traced here: 173 us
  waiting for transfers between devices  142 us (82%)
  between operations  13.8 us (8%)
  matrix products  12.1 us (7%)
  other arithmetic  3.33 us (2%)
    reduce_scatter x1, waiting for transfers between devices, body(): lax.psum_scatter(lax.dot_general(kback, tokens, (((0,), (0,)), ((), ())),...  66.6 us
    all_gather x1, waiting for transfers between devices, body(): weights = lax.all_gather(key_weight, 'fsdp', axis=0, tiled=True)  40.1 us
    psum x1, waiting for transfers between devices, body(): kraw = lax.psum(partial_value, 'tensor')  35 us
    dot_general x1, matrix products, body(): lax.dot_general(kback, tokens, (((0,), (0,)), ((), ())), preferred_elemen...  4.5 us
    dot_general x1, matrix products, body(): grad_tokens = jnp.dot(kback, weights, preferred_element_type=jnp.float32)  3.88 us
    dot_general x1, matrix products, body(): lax.dot_general(tokens, weights, (((1,), (1,)), ((), ())), preferred_elem...  3.71 us
  transfers between devices with their start and end apart: 3, of which 3 were waited for; matrix products, arithmetic and copies ran while one was open for 4% of the time, Pallas kernels for 0%

commit v1 on v0

--- a/solution.py
+++ b/solution.py
@@ -1,9 +1,17 @@
+import functools
+
 import jax
 import jax.numpy as jnp
+import numpy as np
 from jax import lax
+from jax.experimental import pallas as pl
+from jax.experimental.pallas import tpu as pltpu
 from jax.sharding import PartitionSpec as P
 
 HEAD = 128
+MESH = pl.DeviceIdType.MESH
+F32 = jnp.float32
+BF16 = jnp.bfloat16
 
 
 def doc_positions(segments):
@@ -30,7 +38,7 @@
     return out.reshape(rows, -1)
 
 
-def body(tokens, seg_ids, key_weight, key_grad):
+def plain_body(tokens, seg_ids, key_weight, key_grad):
     cosine, sine = angles(doc_positions(seg_ids[0]), HEAD // 2)
     weights = lax.all_gather(key_weight, "fsdp", axis=0, tiled=True)
     partial_value = lax.dot_general(
@@ -51,7 +59,255 @@
     return (keys, grad_tokens.astype(jnp.bfloat16), grad_key_weight)
 
 
+def turned(block, cosine, signed_sine):
+    return block * cosine + pltpu.roll(block, HEAD // 2, 1) * signed_sine
+
+
+def cube_kernel(
+    nz, tile,
+    tok, seg, w, kg, freq,
+    keys_out, gtok_out, gw_out,
+    wall, tok_sib, kbt, kbt_sib, kb, cos_s, sin_s, snd, comb, from_x, from_y, fin_x, fin_y,
+    kraw, zin, keyb,
+    s_ag, r_ag, s_sib, r_sib, s_rs, r_rs, s_z, r_z, s_k, r_k,
+):
+    f, t = lax.axis_index("fsdp"), lax.axis_index("tensor")
+    y, x, c = f // 4, (f // 2) % 2, f % 2
+    xn = y * 4 + (1 - x) * 2 + c
+    yn = (1 - y) * 4 + x * 2 + c
+    dg = (1 - y) * 4 + (1 - x) * 2 + c
+    sib = y * 4 + x * 2 + (1 - c)
+    rows, depth = w.shape
+    half = rows // 2
+    toks, heads = tok.shape[0], kg.shape[1] // HEAD
+    peers = [lax.rem(t + d, nz) for d in range(1, nz)]
+
+    barrier = pltpu.get_barrier_semaphore()
+    for g in (xn, yn, sib):
+        pl.semaphore_signal(barrier, inc=1, device_id=(g, t), device_id_type=MESH)
+    for p in peers:
+        pl.semaphore_signal(barrier, inc=1, device_id=(f, p), device_id_type=MESH)
+    pl.semaphore_wait(barrier, 3 + len(peers))
+
+    pending = []
+
+    def send(src, dst, ssem, rsem, g, p):
+        copy = pltpu.make_async_remote_copy(
+            src_ref=src, dst_ref=dst, send_sem=ssem, recv_sem=rsem,
+            device_id=(g, p), device_id_type=MESH,
+        )
+        copy.start()
+        pending.append(copy)
+        return copy
+
+    def shard_half(g, h):
+        return wall.at[pl.ds(pl.multiple_of(g * rows + h * half, half), half)]
+
+    def w_half(h):
+        return w.at[pl.ds(h * half, half)]
+
+    ax, ay = [None, None], [None, None]
+    ax[0] = send(w_half(0), shard_half(f, 0), s_ag.at[0], r_ag.at[0], xn, t)
+    ay[1] = send(w_half(1), shard_half(f, 1), s_ag.at[3], r_ag.at[3], yn, t)
+    tok_copy = send(tok, tok_sib, s_sib.at[0], r_sib.at[0], sib, t)
+    ax[1] = send(w_half(1), shard_half(f, 1), s_ag.at[1], r_ag.at[1], xn, t)
+    ay[0] = send(w_half(0), shard_half(f, 0), s_ag.at[2], r_ag.at[2], yn, t)
+    own_rows = pl.ds(pl.multiple_of(f * rows, rows), rows)
+    own_copy = send(w, wall.at[own_rows], s_sib.at[2], r_sib.at[2], sib, t)
+
+    ids = jnp.broadcast_to(seg[...].astype(F32), (toks, toks))
+    row = lax.broadcasted_iota(jnp.int32, (toks, toks), 0)
+    col = lax.broadcasted_iota(jnp.int32, (toks, toks), 1)
+    same = jnp.where((ids == ids.T) & (col < row), 1.0, 0.0)
+    position = jnp.sum(same, axis=1, keepdims=True)
+    turn = position * freq[...]
+    lane = lax.broadcasted_iota(jnp.int32, (toks, HEAD), 1)
+    cosine = jnp.cos(turn)
+    sine = jnp.sin(turn)
+    sine = jnp.where(lane < HEAD // 2, -sine, sine)
+    cos_s[...] = cosine
+    sin_s[...] = sine
+    for h in range(heads):
+        lanes = pl.ds(h * HEAD, HEAD)
+        back = turned(kg[:, lanes].astype(F32), cosine, -sine).astype(BF16)
+        kb[:, lanes] = back
+        kbt[lanes, :] = back.astype(F32).T.astype(BF16)
+    kb_copy = send(kbt, kbt_sib, s_sib.at[1], r_sib.at[1], sib, t)
+    wall[own_rows, :] = w[...]
+
+    tok_copy.wait_recv()
+    kb_copy.wait_recv()
+    picked = []
+    for g in (dg, xn, yn, f):
+        at = pl.ds(pl.multiple_of(g * rows, rows), rows)
+        picked.append(jnp.concatenate([kbt[at, :], kbt_sib[at, :]], axis=1))
+    left = jnp.concatenate(picked, axis=0)
+
+    @pl.loop(0, depth // tile)
+    def _(i):
+        lanes = pl.ds(pl.multiple_of(i * tile, tile), tile)
+        right = jnp.concatenate([tok[:, lanes], tok_sib[:, lanes]], axis=0)
+        part = jnp.dot(left, right, preferred_element_type=F32)
+        snd[0, :, lanes] = part[:rows].astype(BF16)
+        snd[1, :half, lanes] = part[rows : rows + half].astype(BF16)
+        comb[0, :, lanes] = part[rows + half : 2 * rows]
+        comb[1, :, lanes] = part[2 * rows : 2 * rows + half]
+        snd[2, half:, lanes] = part[2 * rows + half : 3 * rows].astype(BF16)
+        gw_out[:, lanes] = part[3 * rows :]
+
+    sib_waits = [own_copy]
+
+    def to_sib(g, h, n):
+        sib_waits.append(
+            send(shard_half(g, h), shard_half(g, h), s_sib.at[n], r_sib.at[n], sib, t)
+        )
+
+    ax[0].wait_recv()
+    ad0 = send(shard_half(xn, 0), shard_half(xn, 0), s_ag.at[4], r_ag.at[4], yn, t)
+    ay[1].wait_recv()
+    ad1 = send(shard_half(yn, 1), shard_half(yn, 1), s_ag.at[5], r_ag.at[5], xn, t)
+    to_sib(xn, 0, 3)
+    to_sib(yn, 1, 4)
+
+    top, bottom = pl.ds(0, half), pl.ds(half, half)
+    rdx = send(snd.at[0, top], from_x, s_rs.at[0], r_rs.at[0], xn, t)
+    rdy = send(snd.at[0, bottom], from_y, s_rs.at[1], r_rs.at[1], yn, t)
+    fx0 = send(snd.at[1, top], fin_x.at[top], s_rs.at[2], r_rs.at[2], xn, t)
+    fy1 = send(snd.at[2, bottom], fin_y.at[bottom], s_rs.at[3], r_rs.at[3], yn, t)
+
+    ax[1].wait_recv()
+    to_sib(xn, 1, 5)
+    ay[0].wait_recv()
+    to_sib(yn, 0, 6)
+    ad0.wait_recv()
+    to_sib(dg, 0, 7)
+    ad1.wait_recv()
+    to_sib(dg, 1, 8)
+    for copy in sib_waits:
+        copy.wait_recv()
+
+    kraw[...] = jnp.zeros_like(kraw)
+
+    @pl.loop(0, depth // tile)
+    def _(i):
+        lanes = pl.ds(pl.multiple_of(i * tile, tile), tile)
+        kraw[...] += lax.dot_general(
+            tok[:, lanes], wall[:, lanes], (((1,), (1,)), ((), ())), preferred_element_type=F32
+        )
+
+    share = toks // nz
+
+    def rows_of(p):
+        return pl.ds(pl.multiple_of(p * share, share), share)
+
+    z_copies = [
+        send(kraw.at[rows_of(p)], zin.at[d], s_z.at[d], r_z.at[d], f, p)
+        for d, p in enumerate(peers)
+    ]
+
+    rdx.wait_recv()
+    snd[2, :half] = (comb[1] + from_x[...].astype(F32)).astype(BF16)
+    fy0 = send(snd.at[2, top], fin_y.at[top], s_rs.at[4], r_rs.at[4], yn, t)
+    rdy.wait_recv()
+    snd[1, half:] = (comb[0] + from_y[...].astype(F32)).astype(BF16)
+    fx1 = send(snd.at[1, bottom], fin_x.at[bottom], s_rs.at[5], r_rs.at[5], xn, t)
+
+    mine = rows_of(t)
+    total = kraw[mine, :]
+    for d, copy in enumerate(z_copies):
+        copy.wait_recv()
+        total = total + zin[d]
+    cosine, sine = cos_s[mine, :], sin_s[mine, :]
+    for h in range(heads):
+        keyb[mine, h * HEAD : (h + 1) * HEAD] = turned(
+            total[:, h * HEAD : (h + 1) * HEAD], cosine, sine
+        ).astype(BF16)
+    k_copies = [
+        send(keyb.at[mine], keyb.at[mine], s_k.at[d], r_k.at[d], f, p)
+        for d, p in enumerate(peers)
+    ]
+
+    @pl.loop(0, depth // tile)
+    def _(i):
+        lanes = pl.ds(pl.multiple_of(i * tile, tile), tile)
+        gtok_out[:, lanes] = jnp.dot(
+            kb[...], wall[:, lanes], preferred_element_type=F32
+        ).astype(BF16)
+
+    for copy in k_copies:
+        copy.wait_recv()
+    keys_out[...] = keyb[...]
+
+    fx0.wait_recv()
+    gw_out[:half] += fin_x[:half].astype(F32)
+    fy1.wait_recv()
+    gw_out[half:] += fin_y[half:].astype(F32)
+    fy0.wait_recv()
+    gw_out[:half] += fin_y[:half].astype(F32)
+    fx1.wait_recv()
+    gw_out[half:] += fin_x[half:].astype(F32)
+    for copy in pending:
+        copy.wait_send()
+
+
+def cube_body(nz, tokens, seg_ids, key_weight, key_grad):
+    toks, depth = tokens.shape
+    rows, width = key_weight.shape[0], key_grad.shape[1]
+    half = rows // 2
+    tile = min(512, depth)
+    freq = np.float32(500000.0) ** (-2.0 * np.arange(HEAD // 2, dtype=np.float32) / HEAD)
+    freq = jnp.asarray(np.tile(freq.astype(np.float32), 2)[None, :])
+    vmem = pl.BlockSpec(memory_space=pltpu.VMEM)
+    dma = pltpu.SemaphoreType.DMA
+    far = max(nz - 1, 1)
+    return pl.pallas_call(
+        functools.partial(cube_kernel, nz, tile),
+        out_shape=(
+            jax.ShapeDtypeStruct((toks, width), BF16),
+            jax.ShapeDtypeStruct((toks, depth), BF16),
+            jax.ShapeDtypeStruct((rows, depth), F32),
+        ),
+        in_specs=[vmem] * 5,
+        out_specs=(vmem,) * 3,
+        scratch_shapes=[
+            pltpu.VMEM((width, depth), BF16),
+            pltpu.VMEM((toks, depth), BF16),
+            pltpu.VMEM((width, toks), BF16),
+            pltpu.VMEM((width, toks), BF16),
+            pltpu.VMEM((toks, width), BF16),
+            pltpu.VMEM((toks, HEAD), F32),
+            pltpu.VMEM((toks, HEAD), F32),
+            pltpu.VMEM((3, rows, depth), BF16),
+            pltpu.VMEM((2, half, depth), F32),
+            pltpu.VMEM((half, depth), BF16),
+            pltpu.VMEM((half, depth), BF16),
+            pltpu.VMEM((rows, depth), BF16),
+            pltpu.VMEM((rows, depth), BF16),
+            pltpu.VMEM((toks, width), F32),
+            pltpu.VMEM((far, toks // nz, width), F32),
+            pltpu.VMEM((toks, width), BF16),
+            dma((6,)), dma((6,)),
+            dma((9,)), dma((9,)),
+            dma((6,)), dma((6,)),
+            dma((far,)), dma((far,)),
+            dma((far,)), dma((far,)),
+        ],
+        compiler_params=pltpu.CompilerParams(
+            collective_id=0, has_side_effects=True, vmem_limit_bytes=40 * 1024 * 1024
+        ),
+        cost_estimate=pl.CostEstimate(
+            flops=6 * toks * width * depth,
+            bytes_accessed=4 * toks * depth + 6 * rows * depth,
+            transcendentals=2 * toks * HEAD,
+        ),
+    )(tokens, seg_ids, key_weight, key_grad, freq)
+
+
 def solution(mesh):
+    nz = mesh.shape["tensor"]
+    body = plain_body
+    if mesh.shape["fsdp"] == 8 and nz <= 8:
+        body = functools.partial(cube_body, nz)
     placed = (P("fsdp", "tensor"), P("fsdp", None), P("fsdp", "tensor"), P("fsdp", None))
     return jax.shard_map(
         body,

time: 174 us -> 49.3 us (0.28)
  waiting for transfers between devices: 142 us -> 0 us
  Pallas kernels: 0 us -> 41.3 us
  between operations: 13.8 us -> 0.65 us
  matrix products: 12.1 us -> 0 us
  local copies, waits for them, and re-layouts: 1.68 us -> 7.07 us
  other arithmetic: 3.33 us -> 0 us
    reduce_scatter x1 -> x0, waiting for transfers between devices: 66.6 us -> none  [body(): lax.psum_scatter(lax.dot_general(kback, tokens, (((0,), (0,)), ((), ())),...]
    pallas_call x0 -> x1, Pallas kernels: none -> 41.3 us  [cube_body(): pl.pallas_call(functools.partial(cube_kernel, nz, tile), out_shape=(jax.S...]
    all_gather x1 -> x0, waiting for transfers between devices: 40.1 us -> none  [body(): weights = lax.all_gather(key_weight, 'fsdp', axis=0, tiled=True)]
    psum x1 -> x0, waiting for transfers between devices: 35 us -> none  [body(): kraw = lax.psum(partial_value, 'tensor')]
    dot_general x3 -> x0, matrix products: 12.1 us -> none  [the longest x1 4.5 us: body(): lax.dot_general(kback, tokens, (((0,), (0,)), ((), ())), preferred_elemen...]
    unnamed x5 -> x13, local copies, waits for them, and re-layouts: 0.69 us -> 7.07 us
    another operation x3 -> x0, other arithmetic: 1.76 us -> none
  transfers between devices with their start and end apart: 3 -> 0, of which waited for: 3 -> 0; matrix products, arithmetic and copies ran while one was open for 4% -> 0% of each run, Pallas kernels for 0% -> 0%
where the time goes in v1:
time: 49.3 us; the launch traced here: 49 us
  Pallas kernels  41.3 us (84%)
  local copies, waits for them, and re-layouts  7.07 us (14%)
  between operations  0.65 us (1%)
    pallas_call x1, Pallas kernels, cube_body(): pl.pallas_call(functools.partial(cube_kernel, nz, tile), out_shape=(jax.S...  41.3 us
    unnamed x13, local copies, waits for them, and re-layouts  7.07 us

profile of v1, /device:TPU:0, one launch (start us, length us, event | category | flops | bytes accessed | tf_op | source)
XLA Modules:
  0.0 49.0 jit_solution(12714984685400561760)
XLA Ops:
  0.6 0.0 copy-start
  0.6 1.2 %copy-done = bf16[128,4096]{1,0:T(8,128)(2,1)S(1)} copy-done((bf16[128,4096]{1,0:T(8,128)(2,1)S(1)}, bf16[128,4096]{1,0:T(8,128)(2,1)}, u32[]{:S(2)}) %copy-start) | copy-done | bytes 1048600
  1.9 0.0 copy-start.1
  1.9 1.0 %copy-done.1 = bf16[64,4096]{1,0:T(8,128)(2,1)S(1)} copy-done((bf16[64,4096]{1,0:T(8,128)(2,1)S(1)}, bf16[64,4096]{1,0:T(8,128)(2,1)}, u32[]{:S(2)}) %copy-start.1) | copy-done | bytes 524312
  2.9 0.0 copy-start.2
  2.9 0.9 %copy-done.2 = bf16[128,512]{1,0:T(8,128)(2,1)S(1)} copy-done((bf16[128,512]{1,0:T(8,128)(2,1)S(1)}, bf16[128,512]{1,0:T(8,128)(2,1)}, u32[]{:S(2)}) %copy-start.2) | copy-done | bytes 131096
  3.8 0.0 copy-start.3
  3.8 0.7 %copy-done.3 = s32[1,128]{1,0:T(1,128)S(1)} copy-done((s32[1,128]{1,0:T(1,128)S(1)}, s32[1,128]{1,0:T(1,128)}, u32[]{:S(2)}) %copy-start.3) | copy-done | bytes 536
  4.5 0.0 copy-start.4
  4.5 0.7 %copy-done.4 = f32[1,128]{1,0:T(1,128)S(1)} copy-done((f32[1,128]{1,0:T(1,128)S(1)}, f32[1,128]{1,0:T(1,128)}, u32[]{:S(2)}) %copy-start.4) | copy-done | bytes 536
  5.1 41.3 %shard_map.76 = (bf16[128,512]{1,0:T(8,128)(2,1)S(1)}, bf16[128,4096]{1,0:T(8,128)(2,1)S(1)}, f32[64,4096]{1,0:T(8,128)S(1)}) custom-call(bf16[128,4096]{1,0:T(8,128)(2,1)S(1)} %copy-done, s32[1,128]{1,0:T(1,128)S(1)} %copy-done.3, bf16[64,4096]{1,0:T(8,128)(2,1)S(1)} %copy-done.1, bf16[128,512]{1,0:T(8,128)(2,1)S(1)} %copy-done.2, f32[1,128]{1,0:T(1,128)S(1)} %copy-done.4), custom_call_target="tpu_custom_call" | custom-call | flops 1610612736 | bytes 3670016 | tf_op jit(solution)/shard_map/pallas_call | solution.py:263
  46.4 0.7 %copy.11 = bf16[128,512]{1,0:T(8,128)(2,1)} copy(bf16[128,512]{1,0:T(8,128)(2,1)S(1)} %get-tuple-element.6) | data formatting | bytes 262144
  47.1 1.0 %copy.12 = bf16[128,4096]{1,0:T(8,128)(2,1)} copy(bf16[128,4096]{1,0:T(8,128)(2,1)S(1)} %get-tuple-element.7) | data formatting | bytes 2097152
  48.1 1.0 %copy.13 = f32[64,4096]{1,0:T(8,128)} copy(f32[64,4096]{1,0:T(8,128)S(1)} %get-tuple-element.8) | data formatting | bytes 2097152
Async XLA Ops:
  0.6 1.2 %copy-start = (bf16[128,4096]{1,0:T(8,128)(2,1)S(1)}, bf16[128,4096]{1,0:T(8,128)(2,1)}, u32[]{:S(2)}) copy-start(bf16[128,4096]{1,0:T(8,128)(2,1)} %tok.1) | copy-start | bytes 3145732
  1.9 1.0 %copy-start.1 = (bf16[64,4096]{1,0:T(8,128)(2,1)S(1)}, bf16[64,4096]{1,0:T(8,128)(2,1)}, u32[]{:S(2)}) copy-start(bf16[64,4096]{1,0:T(8,128)(2,1)} %w.1) | copy-start | bytes 1572868
  2.9 0.9 %copy-start.2 = (bf16[128,512]{1,0:T(8,128)(2,1)S(1)}, bf16[128,512]{1,0:T(8,128)(2,1)}, u32[]{:S(2)}) copy-start(bf16[128,512]{1,0:T(8,128)(2,1)} %kg.1) | copy-start | bytes 393220
  3.8 0.7 %copy-start.3 = (s32[1,128]{1,0:T(1,128)S(1)}, s32[1,128]{1,0:T(1,128)}, u32[]{:S(2)}) copy-start(s32[1,128]{1,0:T(1,128)} %seg.1) | copy-start | bytes 1540
  4.5 0.7 %copy-start.4 = (f32[1,128]{1,0:T(1,128)S(1)}, f32[1,128]{1,0:T(1,128)}, u32[]{:S(2)}) copy-start(f32[1,128]{1,0:T(1,128)} %constant.2.clone.freq) | copy-start | bytes 1540

commit v2 on v1

--- a/solution.py
+++ b/solution.py
@@ -65,11 +65,11 @@
 
 def cube_kernel(
     nz, tile,
-    tok, seg, w, kg, freq,
-    keys_out, gtok_out, gw_out,
-    wall, tok_sib, kbt, kbt_sib, kb, cos_s, sin_s, snd, comb, from_x, from_y, fin_x, fin_y,
-    kraw, zin, keyb,
-    s_ag, r_ag, s_sib, r_sib, s_rs, r_rs, s_z, r_z, s_k, r_k,
+    tok_hbm, seg_hbm, w, kg_hbm, freq_hbm,
+    keys_hbm, gtok_hbm, gw_hbm,
+    keyb, gtok_out, gw_out, tok, seg, kg, freq, wall, tok_sib, kbt, kbt_sib, kb, cos_s, sin_s, snd, comb, from_x, from_y, fin_x, fin_y,
+    kraw, zin,
+    s_ag, r_ag, s_sib, r_sib, s_rs, r_rs, s_z, r_z, s_k, r_k, s_in, s_out,
 ):
     f, t = lax.axis_index("fsdp"), lax.axis_index("tensor")
     y, x, c = f // 4, (f // 2) % 2, f % 2
@@ -87,6 +87,15 @@
         pl.semaphore_signal(barrier, inc=1, device_id=(g, t), device_id_type=MESH)
     for p in peers:
         pl.semaphore_signal(barrier, inc=1, device_id=(f, p), device_id_type=MESH)
+    own_rows = pl.ds(pl.multiple_of(f * rows, rows), rows)
+    loads = [
+        pltpu.make_async_copy(src, dst, s_in.at[n])
+        for n, (src, dst) in enumerate(
+            ((seg_hbm, seg), (freq_hbm, freq), (kg_hbm, kg), (tok_hbm, tok), (w, wall.at[own_rows]))
+        )
+    ]
+    for load in loads:
+        load.start()
     pl.semaphore_wait(barrier, 3 + len(peers))
 
     pending = []
@@ -109,12 +118,13 @@
     ax, ay = [None, None], [None, None]
     ax[0] = send(w_half(0), shard_half(f, 0), s_ag.at[0], r_ag.at[0], xn, t)
     ay[1] = send(w_half(1), shard_half(f, 1), s_ag.at[3], r_ag.at[3], yn, t)
-    tok_copy = send(tok, tok_sib, s_sib.at[0], r_sib.at[0], sib, t)
+    tok_copy = send(tok_hbm, tok_sib, s_sib.at[0], r_sib.at[0], sib, t)
     ax[1] = send(w_half(1), shard_half(f, 1), s_ag.at[1], r_ag.at[1], xn, t)
     ay[0] = send(w_half(0), shard_half(f, 0), s_ag.at[2], r_ag.at[2], yn, t)
-    own_rows = pl.ds(pl.multiple_of(f * rows, rows), rows)
     own_copy = send(w, wall.at[own_rows], s_sib.at[2], r_sib.at[2], sib, t)
 
+    for load in loads[:3]:
+        load.wait()
     ids = jnp.broadcast_to(seg[...].astype(F32), (toks, toks))
     row = lax.broadcasted_iota(jnp.int32, (toks, toks), 0)
     col = lax.broadcasted_iota(jnp.int32, (toks, toks), 1)
@@ -133,8 +143,9 @@
         kb[:, lanes] = back
         kbt[lanes, :] = back.astype(F32).T.astype(BF16)
     kb_copy = send(kbt, kbt_sib, s_sib.at[1], r_sib.at[1], sib, t)
-    wall[own_rows, :] = w[...]
-
+
+    for load in loads[3:]:
+        load.wait()
     tok_copy.wait_recv()
     kb_copy.wait_recv()
     picked = []
@@ -234,9 +245,12 @@
             kb[...], wall[:, lanes], preferred_element_type=F32
         ).astype(BF16)
 
+    moves = [pltpu.make_async_copy(gtok_out, gtok_hbm, s_out.at[0])]
+    moves[0].start()
     for copy in k_copies:
         copy.wait_recv()
-    keys_out[...] = keyb[...]
+    moves.append(pltpu.make_async_copy(keyb, keys_hbm, s_out.at[1]))
+    moves[1].start()
 
     fx0.wait_recv()
     gw_out[:half] += fin_x[:half].astype(F32)
@@ -244,10 +258,27 @@
     gw_out[half:] += fin_y[half:].astype(F32)
     fy0.wait_recv()
     gw_out[:half] += fin_y[:half].astype(F32)
+    moves.append(pltpu.make_async_copy(gw_out.at[top], gw_hbm.at[top], s_out.at[2]))
+    moves[2].start()
     fx1.wait_recv()
     gw_out[half:] += fin_x[half:].astype(F32)
+    moves.append(pltpu.make_async_copy(gw_out.at[bottom], gw_hbm.at[bottom], s_out.at[3]))
+    moves[3].start()
+    for copy in moves:
+        copy.wait()
     for copy in pending:
         copy.wait_send()
+
+
+def move_out(keys, gtok, gw, keys_out, gtok_out, gw_out, sem):
+    copies = [
+        pltpu.make_async_copy(src, dst, sem.at[n])
+        for n, (src, dst) in enumerate(((keys, keys_out), (gtok, gtok_out), (gw, gw_out)))
+    ]
+    for copy in copies:
+        copy.start()
+    for copy in copies:
+        copy.wait()
 
 
 def cube_body(nz, tokens, seg_ids, key_weight, key_grad):
@@ -257,19 +288,28 @@
     tile = min(512, depth)
     freq = np.float32(500000.0) ** (-2.0 * np.arange(HEAD // 2, dtype=np.float32) / HEAD)
     freq = jnp.asarray(np.tile(freq.astype(np.float32), 2)[None, :])
-    vmem = pl.BlockSpec(memory_space=pltpu.VMEM)
+    limit = 60 * 1024 * 1024
+    hbm = pl.BlockSpec(memory_space=pltpu.HBM)
     dma = pltpu.SemaphoreType.DMA
     far = max(nz - 1, 1)
-    return pl.pallas_call(
+    shapes = (
+        jax.ShapeDtypeStruct((toks, width), BF16),
+        jax.ShapeDtypeStruct((toks, depth), BF16),
+        jax.ShapeDtypeStruct((rows, depth), F32),
+    )
+    results = pl.pallas_call(
         functools.partial(cube_kernel, nz, tile),
-        out_shape=(
-            jax.ShapeDtypeStruct((toks, width), BF16),
-            jax.ShapeDtypeStruct((toks, depth), BF16),
-            jax.ShapeDtypeStruct((rows, depth), F32),
-        ),
-        in_specs=[vmem] * 5,
-        out_specs=(vmem,) * 3,
+        out_shape=shapes,
+        in_specs=[hbm] * 5,
+        out_specs=(hbm,) * 3,
         scratch_shapes=[
+            pltpu.VMEM((toks, width), BF16),
+            pltpu.VMEM((toks, depth), BF16),
+            pltpu.VMEM((rows, depth), F32),
+            pltpu.VMEM((toks, depth), BF16),
+            pltpu.VMEM(seg_ids.shape, jnp.int32),
+            pltpu.VMEM(key_grad.shape, BF16),
+            pltpu.VMEM(freq.shape, F32),
             pltpu.VMEM((width, depth), BF16),
             pltpu.VMEM((toks, depth), BF16),
             pltpu.VMEM((width, toks), BF16),
@@ -285,15 +325,15 @@
             pltpu.VMEM((rows, depth), BF16),
             pltpu.VMEM((toks, width), F32),
             pltpu.VMEM((far, toks // nz, width), F32),
-            pltpu.VMEM((toks, width), BF16),
             dma((6,)), dma((6,)),
             dma((9,)), dma((9,)),
             dma((6,)), dma((6,)),
             dma((far,)), dma((far,)),
             dma((far,)), dma((far,)),
+            dma((5,)), dma((4,)),
         ],
         compiler_params=pltpu.CompilerParams(
-            collective_id=0, has_side_effects=True, vmem_limit_bytes=40 * 1024 * 1024
+            collective_id=0, has_side_effects=True, vmem_limit_bytes=limit
         ),
         cost_estimate=pl.CostEstimate(
             flops=6 * toks * width * depth,
@@ -301,6 +341,17 @@
             transcendentals=2 * toks * HEAD,
         ),
     )(tokens, seg_ids, key_weight, key_grad, freq)
+    return pl.pallas_call(
+        move_out,
+        out_shape=shapes,
+        in_specs=[hbm] * 3,
+        out_specs=(hbm,) * 3,
+        scratch_shapes=[dma((3,))],
+        compiler_params=pltpu.CompilerParams(vmem_limit_bytes=limit),
+        cost_estimate=pl.CostEstimate(
+            flops=0, bytes_accessed=2 * toks * depth + 4 * rows * depth, transcendentals=0
+        ),
+    )(*results)
 
 
 def solution(mesh):

time: 49.3 us -> 112 us (2.27)
  Pallas kernels: 41.3 us -> 111 us
  local copies, waits for them, and re-layouts: 7.07 us -> 0 us
    pallas_call x1 -> x2, Pallas kernels: 41.3 us -> 111 us  [the longest x1 68.6 us: cube_body(): pl.pallas_call(move_out, out_shape=shapes, in_specs=[hbm] * 3, out_specs=...]
    unnamed x13 -> x0, local copies, waits for them, and re-layouts: 7.07 us -> none
where the time goes in v2:
time: 112 us
  Pallas kernels  111 us (99%)
    pallas_call x1, Pallas kernels, cube_body(): pl.pallas_call(move_out, out_shape=shapes, in_specs=[hbm] * 3, out_specs=...  68.6 us
    pallas_call x1, Pallas kernels, cube_body(): pl.pallas_call(functools.partial(cube_kernel, nz, tile), out_shape=shapes...  42.6 us

profile of v2, /device:TPU:0, one launch (start us, length us, event | category | flops | bytes accessed | tf_op | source)
XLA Modules:
  0.0 111.9 jit_solution(8023458445576423792)
XLA Ops:
  0.6 42.6 %shard_map.76 = (bf16[128,512]{1,0:T(8,128)(2,1)}, bf16[128,4096]{1,0:T(8,128)(2,1)}, f32[64,4096]{1,0:T(8,128)}) custom-call(bf16[128,4096]{1,0:T(8,128)(2,1)} %tok_hbm.1, s32[1,128]{1,0:T(1,128)} %seg_hbm.1, bf16[64,4096]{1,0:T(8,128)(2,1)} %w.1, bf16[128,512]{1,0:T(8,128)(2,1)} %kg_hbm.1, f32[1,128]{1,0:T(1,128)} %constant.2.clone.freq_hbm), custom_call_target="tpu_custom_call" | custom-call | flops 1610612736 | bytes 3670016 | tf_op jit(solution)/shard_map/pallas_call | solution.py:300
  43.3 68.6 %shard_map.77 = (bf16[128,512]{1,0:T(8,128)(2,1)}, bf16[128,4096]{1,0:T(8,128)(2,1)}, f32[64,4096]{1,0:T(8,128)}) custom-call(bf16[128,512]{1,0:T(8,128)(2,1)} %get-tuple-element.6.keys, bf16[128,4096]{1,0:T(8,128)(2,1)} %get-tuple-element.7.gtok, f32[64,4096]{1,0:T(8,128)} %get-tuple-element.8.gw), custom_call_target="tpu_custom_call" | custom-call | bytes 2097152 | tf_op jit(solution)/shard_map/pallas_call | solution.py:344

commit v3 on v2

--- a/solution.py
+++ b/solution.py
@@ -180,16 +180,16 @@
     to_sib(xn, 0, 3)
     to_sib(yn, 1, 4)
 
+    ax[1].wait_recv()
+    to_sib(xn, 1, 5)
+    ay[0].wait_recv()
+    to_sib(yn, 0, 6)
     top, bottom = pl.ds(0, half), pl.ds(half, half)
     rdx = send(snd.at[0, top], from_x, s_rs.at[0], r_rs.at[0], xn, t)
     rdy = send(snd.at[0, bottom], from_y, s_rs.at[1], r_rs.at[1], yn, t)
     fx0 = send(snd.at[1, top], fin_x.at[top], s_rs.at[2], r_rs.at[2], xn, t)
     fy1 = send(snd.at[2, bottom], fin_y.at[bottom], s_rs.at[3], r_rs.at[3], yn, t)
 
-    ax[1].wait_recv()
-    to_sib(xn, 1, 5)
-    ay[0].wait_recv()
-    to_sib(yn, 0, 6)
     ad0.wait_recv()
     to_sib(dg, 0, 7)
     ad1.wait_recv()
@@ -270,14 +270,16 @@
         copy.wait_send()
 
 
-def move_out(keys, gtok, gw, keys_out, gtok_out, gw_out, sem):
-    copies = [
-        pltpu.make_async_copy(src, dst, sem.at[n])
-        for n, (src, dst) in enumerate(((keys, keys_out), (gtok, gtok_out), (gw, gw_out)))
-    ]
-    for copy in copies:
+def move_out(keys, gtok, gw, keys_out, gtok_out, gw_out, keys_v, gtok_v, gw_v, s_in, s_out):
+    whole = ((gw, gw_v, gw_out), (gtok, gtok_v, gtok_out), (keys, keys_v, keys_out))
+    ins = [pltpu.make_async_copy(a, v, s_in.at[n]) for n, (a, v, _) in enumerate(whole)]
+    outs = [pltpu.make_async_copy(v, b, s_out.at[n]) for n, (_, v, b) in enumerate(whole)]
+    for copy in ins:
         copy.start()
-    for copy in copies:
+    for arrived, leaving in zip(ins, outs):
+        arrived.wait()
+        leaving.start()
+    for copy in outs:
         copy.wait()
 
 
@@ -346,7 +348,7 @@
         out_shape=shapes,
         in_specs=[hbm] * 3,
         out_specs=(hbm,) * 3,
-        scratch_shapes=[dma((3,))],
+        scratch_shapes=[pltpu.VMEM(a.shape, a.dtype) for a in shapes] + [dma((3,)), dma((3,))],
         compiler_params=pltpu.CompilerParams(vmem_limit_bytes=limit),
         cost_estimate=pl.CostEstimate(
             flops=0, bytes_accessed=2 * toks * depth + 4 * rows * depth, transcendentals=0

time: 112 us -> 46.1 us (0.41)
  Pallas kernels: 111 us -> 45.3 us
    pallas_call x1, Pallas kernels: 68.6 us -> 2.62 us  [cube_body(): pl.pallas_call(move_out, out_shape=shapes, in_specs=[hbm] * 3, out_specs=...]
where the time goes in v3:
time: 46.1 us; the launch traced here: 45.9 us
  Pallas kernels  45.3 us (98%)
  between operations  0.64 us (1%)
    pallas_call x1, Pallas kernels, cube_body(): pl.pallas_call(functools.partial(cube_kernel, nz, tile), out_shape=shapes...  42.6 us
    pallas_call x1, Pallas kernels, cube_body(): pl.pallas_call(move_out, out_shape=shapes, in_specs=[hbm] * 3, out_specs=...  2.62 us

profile of v3, /device:TPU:0, one launch (start us, length us, event | category | flops | bytes accessed | tf_op | source)
XLA Modules:
  0.0 45.9 jit_solution(6652995128774651961)
XLA Ops:
  0.6 42.6 %shard_map.76 = (bf16[128,512]{1,0:T(8,128)(2,1)}, bf16[128,4096]{1,0:T(8,128)(2,1)}, f32[64,4096]{1,0:T(8,128)}) custom-call(bf16[128,4096]{1,0:T(8,128)(2,1)} %tok_hbm.1, s32[1,128]{1,0:T(1,128)} %seg_hbm.1, bf16[64,4096]{1,0:T(8,128)(2,1)} %w.1, bf16[128,512]{1,0:T(8,128)(2,1)} %kg_hbm.1, f32[1,128]{1,0:T(1,128)} %constant.2.clone.freq_hbm), custom_call_target="tpu_custom_call" | custom-call | flops 1610612736 | bytes 3670016 | tf_op jit(solution)/shard_map/pallas_call | solution.py:302
  43.3 2.6 %shard_map.77 = (bf16[128,512]{1,0:T(8,128)(2,1)}, bf16[128,4096]{1,0:T(8,128)(2,1)}, f32[64,4096]{1,0:T(8,128)}) custom-call(bf16[128,512]{1,0:T(8,128)(2,1)} %get-tuple-element.6.keys, bf16[128,4096]{1,0:T(8,128)(2,1)} %get-tuple-element.7.gtok, f32[64,4096]{1,0:T(8,128)} %get-tuple-element.8.gw), custom_call_target="tpu_custom_call" | custom-call | bytes 2097152 | tf_op jit(solution)/shard_map/pallas_call | solution.py:346
